TPU v7x, 32 devices: a whole 2x2x4 slice. The times are simulated.
32 devices in a mesh: grp: 4 (over z), dev: 8 (over y, x, core).
Axes of the slice: x: 2, y: 2, z: 4, core: 2. Of those that a mesh axis runs over, the one named last changes fastest.
Arguments:
- columns: float32 [16384, 768], P(('grp', 'dev')), may hold values from -6 to 6
- points: float32 [3, 16384], P(None, ('grp', 'dev')), may hold values from 0 to 1, as said below
- basis: float32 [16384, 128], P(('grp', 'dev')), may hold values from -0.25 to 0.25
- transfer: float32 [32, 128, 128], P(('grp', 'dev')), may hold values from -0.5 to 0.5
- leaf_coupling: float32 [32, 4, 128, 128], P(('grp', 'dev')), may hold values from -0.5 to 0.5
- group_coupling: float32 [4, 4, 128, 128], P('grp', None, 'dev'), may hold values from -0.25 to 0.25
- near_pairs: int32 [32, 3], replicated, may hold values from 0 to 1, as said below
- far_mask: int32 [32, 4], P(('grp', 'dev')), may hold values 0 or 1
- group_link_mask: int32 [4, 4], P('grp'), may hold values 0 or 1
Outputs:
- product: float32 [16384, 768], P(('grp', 'dev'))
Inputs may be any that keep to these rules, and one draw needn't show every extreme that they name: `near_pairs`: each row is a run of ones followed by zeros; some row is all ones. First coordinate of leaf i's points lies in [i / 32, (i + 1) / 32); all coordinates lie in [0, 1).
All inputs are finite; a program needn't handle non-finite values. No bound on the sum of `far_mask` or of `group_link_mask` on one device may be relied on, other than what follows from the above.
Results may differ from a plain program's by a relative error of at most 0.0003.
Values sent between devices are 32-bit elements; how exact they have to be, the bound alone decides.
A program may use at most 64 MiB of HBM per device.

v0:
```python
import functools
import math

import jax
import jax.numpy as jnp
from jax import lax
from jax.experimental import pallas as pl
from jax.experimental.pallas import tpu as pltpu
from jax.sharding import PartitionSpec as P

soften_sq = 0.0025
chunks = 8
row_tile = 128
f32 = jnp.float32
MESH = pl.DeviceIdType.MESH


def slot_of(offset):
    return offset + 3 if offset < 0 else offset + 2


def halves(value):
    high = value.astype(jnp.bfloat16)
    return high, (value - high.astype(f32)).astype(jnp.bfloat16)


def dot16(left, right):
    return jnp.dot(left, right, preferred_element_type=f32)


def dot_split(left, right):
    lh, ll = left
    rh, rl = right
    return dot16(lh, rh) + dot16(lh, rl) + dot16(ll, rh)


def dot16_t(left, right):
    return lax.dot_general(left, right, (((0,), (0,)), ((), ())), preferred_element_type=f32)


def dot_split_t(left, right):
    lh, ll = left
    rh, rl = right
    return dot16_t(lh, rh) + dot16_t(lh, rl) + dot16_t(ll, rh)


def body(
    groups, peers, near_pairs, far_mask, link_mask, cols, pts, basis_in, up_in, coupling_in,
    links_in, out, own, basis, up, coupling, links, slots, xh, xl, pts_t, pown, pbuf, coef, cbuf,
    lift, lift_in, lift_mid, lift_far, gath, part, part_in, part_mid, part_far, far,
    load_sem, s_send, s_recv, p_send, p_recv, c_send, c_recv, pair_send, pair_recv,
    r_send, r_recv, g_send, g_recv, q_send, q_recv, f_send, f_recv,
):
    leaf, width = cols.shape
    loads = [
        pltpu.make_async_copy(source, target, load_sem.at[n])
        for n, (source, target) in enumerate(
            ((cols, own), (basis_in, basis), (up_in, up), (coupling_in, coupling),
             (links_in, links))
        )
    ]
    for load in loads:
        load.start()
    leaves = groups * peers
    grp, dev = lax.axis_index("grp"), lax.axis_index("dev")
    me = grp * peers + dev
    place = lax.rem(me, 4)
    outer = (place == 0) | (place == 3)
    inner = (place == 1) | (place == 2)
    sign = 1 - 2 * (place // 2)
    step = leaf // chunks

    def device(index):
        index = lax.rem(index + leaves, leaves)
        return (index // peers, lax.rem(index, peers))

    barrier = pltpu.get_barrier_semaphore()
    for offset in (-8, -4, -3, -2, -1, 1, 2, 3, 4, 8):
        pl.semaphore_signal(barrier, inc=1, device_id=device(me + offset), device_id_type=MESH)

    @pl.loop(1, peers)
    def _(t):
        pl.semaphore_signal(
            barrier, inc=1, device_id=(grp, lax.rem(dev + t, peers)), device_id_type=MESH
        )

    @pl.loop(1, groups)
    def _(t):
        pl.semaphore_signal(
            barrier, inc=1, device_id=(lax.rem(grp + t, groups), dev), device_id_type=MESH
        )

    pl.semaphore_wait(barrier, 10 + peers - 1 + groups - 1)

    def piece(k):
        return pl.ds(pl.multiple_of(k * step, step), step)

    def relay(source, k, channel, to, offset):
        slot = slot_of(offset)
        return pltpu.make_async_remote_copy(
            src_ref=source.at[piece(k)],
            dst_ref=slots.at[slot, piece(k)],
            send_sem=s_send.at[channel, k],
            recv_sem=s_recv.at[slot, k],
            device_id=device(me + to * sign),
            device_id_type=MESH,
        )

    def arrived(slot, k):
        pltpu.make_async_remote_copy(
            src_ref=cols.at[piece(k)],
            dst_ref=slots.at[slot, piece(k)],
            send_sem=s_send.at[0, k],
            recv_sem=s_recv.at[slot, k],
            device_id=device(me + 1),
            device_id_type=MESH,
        ).wait_recv()

    def arrived_all(slot):
        @pl.loop(0, chunks)
        def _(k):
            arrived(slot, k)

    def own_outer(k):
        return (
            relay(cols, k, 0, 2, 2),
            relay(cols, k, 1, -3, 3),
            relay(cols, k, 2, 1, -1),
        )

    def own_inner(k):
        return (
            relay(cols, k, 0, 2, 2),
            relay(cols, k, 1, 3, -3),
            relay(cols, k, 2, -1, 1),
        )

    plus2, plus3 = slots.at[slot_of(2)], slots.at[slot_of(3)]
    minus1, minus2 = slots.at[slot_of(-1)], slots.at[slot_of(-2)]

    def first_outer(k):
        return relay(plus2, k, 3, 4, -2), relay(plus2, k, 4, 1, 1)

    def first_inner(k):
        return relay(plus3, k, 3, 2, -1), relay(plus2, k, 4, -1, 3)

    def later_outer(k):
        return relay(minus2, k, 5, 1, -3), relay(minus1, k, 6, 1, -2)

    def start_each(copies):
        for copy in copies:
            copy.start()

    def own_start(begin, end):
        @pl.when(outer)
        def _():
            @pl.loop(begin, end)
            def _(k):
                start_each(own_outer(k))

        @pl.when(inner)
        def _():
            @pl.loop(begin, end)
            def _(k):
                start_each(own_inner(k))

    ahead = 2
    own_start(0, ahead)
    pown[0:3, :] = pts[...]
    pown[3:8, :] = jnp.zeros((5, leaf), f32)

    def point_copy(offset):
        return pltpu.make_async_remote_copy(
            src_ref=pown,
            dst_ref=pbuf.at[slot_of(-offset)],
            send_sem=p_send.at[slot_of(offset)],
            recv_sem=p_recv.at[slot_of(-offset)],
            device_id=device(me + offset),
            device_id_type=MESH,
        )

    near_offsets = (-3, -2, -1, 1, 2, 3)
    for offset in near_offsets:
        point_copy(offset).start()

    def split_columns(source):
        @pl.loop(0, leaf // row_tile)
        def _(t):
            rows = pl.ds(pl.multiple_of(t * row_tile, row_tile), row_tile)
            high, low = halves(source[rows, :])
            xh[rows, :] = high
            xl[rows, :] = low

    loads[0].wait()
    split_columns(own)
    loads[1].wait()
    coef[...] = dot_split_t(halves(basis[...]), (xh[...], xl[...]))

    odd = lax.rem(me // 4, 2)
    toward = 4 - 8 * odd

    def coef_copy(source, channel, slot, to):
        return pltpu.make_async_remote_copy(
            src_ref=source,
            dst_ref=cbuf.at[slot],
            send_sem=c_send.at[channel],
            recv_sem=c_recv.at[slot],
            device_id=device(me + to),
            device_id_type=MESH,
        )

    coef_copies = (
        coef_copy(coef, 0, odd, toward),
        coef_copy(cbuf.at[1 - odd], 1, odd, 2 * toward),
        coef_copy(cbuf.at[0], 2, 2, 1),
        coef_copy(cbuf.at[1], 3, 3, -1),
    )
    coef_copies[0].start()

    def coef_arrived(slot):
        coef_copy(coef, 0, slot, 1).wait_recv()

    core, chip, chips = lax.rem(dev, 2), dev // 2, peers // 2
    other = dev + 1 - 2 * core

    def pair_copy(channel, source, target):
        return pltpu.make_async_remote_copy(
            src_ref=source,
            dst_ref=target,
            send_sem=pair_send.at[channel],
            recv_sem=pair_recv.at[channel],
            device_id=(grp, other),
            device_id_type=MESH,
        )

    pair_copies = (
        pair_copy(0, lift.at[1 - core], lift_in),
        pair_copy(1, part.at[1 - core], part_in),
        pair_copy(2, far.at[core], far.at[core]),
    )

    def spread(source, target, send, recv, t):
        to = lax.rem(chip + t, chips)
        return pltpu.make_async_remote_copy(
            src_ref=source.at[to],
            dst_ref=target.at[chip],
            send_sem=send.at[t],
            recv_sem=recv.at[chip],
            device_id=(grp, 2 * to + core),
            device_id_type=MESH,
        )

    def collect(source, target, send, recv, t):
        origin = lax.rem(chip - t + chips, chips)
        pltpu.make_async_remote_copy(
            src_ref=source.at[0],
            dst_ref=target.at[origin],
            send_sem=send.at[0],
            recv_sem=recv.at[origin],
            device_id=(grp, 2 * origin + core),
            device_id_type=MESH,
        ).wait_recv()
        return target[origin]

    def scatter_pair(value, source, channel):
        value = value.reshape((chips, 2) + source.shape[2:])
        for which in range(2):
            source[which] = value[:, which]
        pair_copies[channel].start()

    def scatter_start(source, arriving, middle, target, send, recv, channel):
        pair_copies[channel].wait_recv()
        middle[...] = source[core] + arriving[...]

        @pl.loop(1, chips)
        def _(t):
            spread(middle, target, send, recv, t).start()

    def scatter_end(middle, target, send, recv):
        return lax.fori_loop(
            1, chips,
            lambda t, total: total + collect(middle, target, send, recv, t), middle[chip],
        )

    def group_copy(t):
        return pltpu.make_async_remote_copy(
            src_ref=gath.at[grp],
            dst_ref=gath.at[grp],
            send_sem=g_send.at[t],
            recv_sem=g_recv.at[grp],
            device_id=(lax.rem(grp + t, groups), dev),
            device_id_type=MESH,
        )

    def group_arrived(t):
        origin = lax.rem(grp - t + groups, groups)
        pltpu.make_async_remote_copy(
            src_ref=gath.at[grp],
            dst_ref=gath.at[origin],
            send_sem=g_send.at[0],
            recv_sem=g_recv.at[origin],
            device_id=(origin, dev),
            device_id_type=MESH,
        ).wait_recv()

    def far_copy(t):
        return pltpu.make_async_remote_copy(
            src_ref=far.at[core, chip],
            dst_ref=far.at[core, chip],
            send_sem=f_send.at[t],
            recv_sem=f_recv.at[chip],
            device_id=(grp, 2 * lax.rem(chip + t, chips) + core),
            device_id_type=MESH,
        )

    def far_arrived(t):
        origin = lax.rem(chip - t + chips, chips)
        pltpu.make_async_remote_copy(
            src_ref=far.at[core, chip],
            dst_ref=far.at[core, origin],
            send_sem=f_send.at[0],
            recv_sem=f_recv.at[origin],
            device_id=(grp, 2 * origin + core),
            device_id_type=MESH,
        ).wait_recv()

    loads[2].wait()
    scatter_pair(dot_split_t(halves(up[...]), halves(coef[...])), lift, 0)
    pts_t[...] = pown[...].T

    def near_product(source, weight, first):
        scale = weight * (1.0 / math.sqrt(leaf))

        @pl.loop(0, leaf // row_tile)
        def _(t):
            rows = pl.ds(pl.multiple_of(t * row_tile, row_tile), row_tile)
            squared = None
            for axis in range(3):
                delta = pts_t[rows, axis : axis + 1] - source[axis : axis + 1, :]
                delta = delta - jnp.floor(delta + 0.5)
                squared = delta * delta if squared is None else squared + delta * delta
            block = halves(lax.rsqrt(squared + soften_sq) * scale)
            value = dot_split(block, (xh[...], xl[...]))
            if first:
                out[rows, :] = value
            else:
                out[rows, :] += value

    near_product(pown, 1.0, True)

    def first_relays(begin, end):
        @pl.when(outer)
        def _():
            @pl.loop(begin, end)
            def _(k):
                arrived(slot_of(2), k)
                start_each(first_outer(k))

        @pl.when(inner)
        def _():
            @pl.loop(begin, end)
            def _(k):
                arrived(slot_of(2), k)
                first_inner(k)[1].start()
                arrived(slot_of(3), k)
                first_inner(k)[0].start()

    def add_block(out_offset, in_offset):
        slot = jnp.where(outer, slot_of(out_offset), slot_of(in_offset))
        offset = jnp.where(outer, out_offset, in_offset) * sign
        place_of = jnp.where(offset < 0, offset + 3, offset + 2)
        row = lax.rem(me + jnp.minimum(offset, 0) + leaves, leaves)
        distance = jnp.maximum(offset, -offset)
        weight = (near_pairs[row, distance - 1] > 0).astype(f32)
        split_columns(slots.at[slot])
        near_product(pbuf.at[place_of], weight, False)

    def wait_for(condition, offset):
        @pl.when(condition)
        def _():
            arrived_all(slot_of(offset))

    def turn(k):
        if k + ahead < chunks:
            own_start(k + ahead, k + ahead + 1)
        first_relays(k, k + 1)

    scatter_start(lift, lift_in, lift_mid, lift_far, r_send, r_recv, 0)
    turn(0)
    gath[grp] = scatter_end(lift_mid, lift_far, r_send, r_recv)

    @pl.loop(1, groups)
    def _(t):
        group_copy(t).start()

    turn(1)
    coef_arrived(1 - odd)
    coef_copies[1].start()

    @pl.loop(1, groups)
    def _(t):
        group_arrived(t)

    for load in loads[3:]:
        load.wait()
    flat = jnp.concatenate(
        [gath[h] * link_mask[0, h].astype(f32) for h in range(groups)], axis=0
    )
    scatter_pair(dot_split_t(halves(links[...]), halves(flat)), part, 1)
    turn(2)
    scatter_start(part, part_in, part_mid, part_far, q_send, q_recv, 1)
    turn(3)
    far[core, chip] = scatter_end(part_mid, part_far, q_send, q_recv)

    @pl.loop(1, chips)
    def _(t):
        far_copy(t).start()

    coef_arrived(odd)
    coef_copies[2].start()
    coef_copies[3].start()
    turn(4)

    @pl.loop(1, chips)
    def _(t):
        far_arrived(t)

    pair_copies[2].start()
    turn(5)
    for offset in near_offsets:
        point_copy(offset).wait()
    wait_for(outer, 1)
    wait_for(inner, -1)
    add_block(1, -1)
    for k in range(6, chunks):
        turn(k)
    add_block(2, 2)

    @pl.when(outer)
    def _():
        @pl.loop(0, chunks)
        def _(k):
            copies = later_outer(k)
            arrived(slot_of(-2), k)
            copies[0].start()
            arrived(slot_of(-1), k)
            copies[1].start()

    wait_for(outer, 3)
    wait_for(inner, 1)
    add_block(3, 1)
    wait_for(outer, -3)
    add_block(-3, 3)

    pair_copies[2].wait_recv()
    for slot in (2, 3):
        coef_arrived(slot)
    raised = jnp.stack([far[0], far[1]], axis=1).reshape(up.shape[1], width)
    total = dot_split(halves(up[...]), halves(raised))
    for entry in range(4):
        total += far_mask[0, entry].astype(f32) * dot_split(halves(coupling[entry]), halves(cbuf[entry]))
    total = halves(total)

    @pl.loop(0, leaf // row_tile)
    def _(t):
        rows = pl.ds(pl.multiple_of(t * row_tile, row_tile), row_tile)
        out[rows, :] += dot_split(halves(basis[rows, :]), total)

    wait_for(inner, -2)
    add_block(-1, -2)
    wait_for(inner, -3)
    add_block(-2, -3)

    for copy in coef_copies + pair_copies:
        copy.wait_send()

    @pl.loop(1, chips)
    def _(t):
        spread(lift_mid, lift_far, r_send, r_recv, t).wait_send()
        spread(part_mid, part_far, q_send, q_recv, t).wait_send()
        far_copy(t).wait_send()

    @pl.loop(1, groups)
    def _(t):
        group_copy(t).wait_send()

    @pl.when(outer)
    def _():
        @pl.loop(0, chunks)
        def _(k):
            for copy in own_outer(k) + first_outer(k) + later_outer(k):
                copy.wait_send()

    @pl.when(inner)
    def _():
        @pl.loop(0, chunks)
        def _(k):
            for copy in own_inner(k) + first_inner(k):
                copy.wait_send()


def per_device(
    columns, points, basis, transfer, leaf_coupling, group_coupling, near_pairs, far_mask,
    group_link_mask,
):
    groups, peers = lax.axis_size("grp"), lax.axis_size("dev")
    leaf, width = columns.shape
    rank = basis.shape[1]
    slice_rows = group_coupling.shape[2]
    padded = -(-slice_rows // 8) * 8
    tall = peers * padded
    fill = padded - slice_rows
    up = transfer[0]
    links = group_coupling[0]
    if fill:
        up = jnp.pad(up.reshape(rank, peers, slice_rows), ((0, 0), (0, 0), (0, fill)))
        links = jnp.pad(
            links.reshape(groups, slice_rows, peers, slice_rows),
            ((0, 0), (0, fill), (0, 0), (0, fill)),
        )
    up = up.reshape(rank, tall)
    links = links.reshape(groups * padded, tall)
    vmem = pl.BlockSpec(memory_space=pltpu.VMEM)
    smem = pl.BlockSpec(memory_space=pltpu.SMEM)
    anywhere = pl.BlockSpec(memory_space=pl.ANY)
    dma = pltpu.SemaphoreType.DMA
    chips = peers // 2
    slab = pltpu.VMEM((chips, padded, width), f32)
    pair = pltpu.VMEM((2, chips, padded, width), f32)
    return pl.pallas_call(
        functools.partial(body, groups, peers),
        out_shape=jax.ShapeDtypeStruct((leaf, width), f32),
        in_specs=[smem] * 3 + [anywhere, vmem] + [anywhere] * 4,
        out_specs=vmem,
        scratch_shapes=[
            pltpu.VMEM((leaf, width), f32),
            pltpu.VMEM((leaf, rank), f32),
            pltpu.VMEM((rank, tall), f32),
            pltpu.VMEM(leaf_coupling.shape[1:], f32),
            pltpu.VMEM((groups * padded, tall), f32),
            pltpu.VMEM((6, leaf, width), f32),
            pltpu.VMEM((leaf, width), jnp.bfloat16),
            pltpu.VMEM((leaf, width), jnp.bfloat16),
            pltpu.VMEM((leaf, 8), f32),
            pltpu.VMEM((8, leaf), f32),
            pltpu.VMEM((6, 8, leaf), f32),
            pltpu.VMEM((rank, width), f32),
            pltpu.VMEM((4, rank, width), f32),
            pair,
            slab,
            slab,
            slab,
            pltpu.VMEM((groups, padded, width), f32),
            pair,
            slab,
            slab,
            slab,
            pair,
            dma((5,)),
            dma((7, chunks)),
            dma((6, chunks)),
            dma((6,)),
            dma((6,)),
            dma((4,)),
            dma((4,)),
            dma((3,)),
            dma((3,)),
            dma((chips,)),
            dma((chips,)),
            dma((groups,)),
            dma((groups,)),
            dma((chips,)),
            dma((chips,)),
            dma((chips,)),
            dma((chips,)),
        ],
        compiler_params=pltpu.CompilerParams(
            collective_id=0, has_side_effects=True, vmem_limit_bytes=48 * 1024 * 1024
        ),
    )(
        near_pairs, far_mask, group_link_mask, columns, points, basis, up, leaf_coupling[0],
        links,
    )


def solution(mesh):
    in_specs = (
        P(("grp", "dev"), None),
        P(None, ("grp", "dev")),
        P(("grp", "dev"), None),
        P(("grp", "dev"), None, None),
        P(("grp", "dev"), None, None, None),
        P("grp", None, "dev", None),
        P(),
        P(("grp", "dev"), None),
        P("grp", None),
    )
    return jax.shard_map(
        per_device, mesh=mesh, in_specs=in_specs, out_specs=P(("grp", "dev"), None),
        check_vma=False,
    )
```

profile of v0, /device:TPU:0, one launch (start us, length us, event | category | flops | bytes accessed | tf_op | source)
XLA Modules:
  0.0 107.9 jit_solution(16449084634891107270)
XLA Ops:
  0.0 0.8 copy.10.near_pairs
  0.8 0.0 copy-start
  0.8 1.4 %copy-done = f32[512,768]{1,0:T(8,128)S(1)} copy-done((f32[512,768]{1,0:T(8,128)S(1)}, f32[512,768]{1,0:T(8,128)}, u32[]{:S(2)}) %copy-start) | copy-done | bytes 1572888
  2.2 0.0 copy-start.1
  2.2 0.9 copy-done.1
  3.1 0.0 copy-start.2
  3.1 0.9 copy-done.2
  4.1 0.0 copy-start.3
  4.1 0.8 copy-done.3
  4.9 0.0 copy-start.4
  4.9 0.8 copy-done.4
  5.7 0.0 copy-start.5
  5.7 0.7 copy-done.5
  6.4 0.0 copy-start.6
  6.4 0.7 copy-done.6
  7.0 0.0 copy-start.7
  7.0 0.7 copy-done.7
  7.7 99.1 %shard_map.91 = f32[512,768]{1,0:T(8,128)S(1)} custom-call(s32[32,3]{1,0:T(8,128)S(1)} %copy.10.near_pairs, s32[1,4]{1,0:T(1,128)S(1)} %copy-done.6, s32[1,4]{1,0:T(1,128)S(1)} %copy-done.7, f32[512,768]{1,0:T(8,128)S(1)} %copy-done, f32[3,512]{1,0:T(4,128)S(1)} %copy-done.5, f32[512,128]{1,0:T(8,128)S(1)} %copy-done.1, f32[128,128]{1,0:T(8,128)S(1)} %bitcast.4, ...), custom_call_target="tpu_custom_call" | custom-call | tf_op jit(solution)/shard_map/pallas_call | solution.py:530
  106.8 1.1 %copy.12 = f32[512,768]{1,0:T(8,128)} copy(f32[512,768]{1,0:T(8,128)S(1)} %shard_map.91) | data formatting | bytes 3145728
Async XLA Ops:
  0.8 1.4 %copy-start = (f32[512,768]{1,0:T(8,128)S(1)}, f32[512,768]{1,0:T(8,128)}, u32[]{:S(2)}) copy-start(f32[512,768]{1,0:T(8,128)} %cols.1) | copy-start | bytes 4718596
  2.2 0.9 copy-start.1
  3.1 0.9 copy-start.2
  4.1 0.8 copy-start.3
  4.9 0.8 copy-start.4
  5.7 0.7 copy-start.5
  6.4 0.7 copy-start.6
  7.0 0.7 copy-start.7
where the time goes:
time: 109 us; the launch traced here: 108 us
  Pallas kernels  99.1 us (91%)
  local copies, waits for them, and re-layouts  8.82 us (8%)
    pallas_call x1, Pallas kernels, per_device(): pl.pallas_call(functools.partial(body, groups, peers), out_shape=jax.Shap...  99.1 us
    unnamed x18, local copies, waits for them, and re-layouts  8.82 us

commit v1 on v0

--- a/solution.py
+++ b/solution.py
@@ -9,7 +9,9 @@
 from jax.sharding import PartitionSpec as P
 
 soften_sq = 0.0025
-chunks = 8
+chunks = 16
+ahead = 4
+lag = 3
 row_tile = 128
 f32 = jnp.float32
 MESH = pl.DeviceIdType.MESH
@@ -45,8 +47,8 @@
 
 
 def body(
-    groups, peers, near_pairs, far_mask, link_mask, cols, pts, basis_in, up_in, coupling_in,
-    links_in, out, own, basis, up, coupling, links, slots, xh, xl, pts_t, pown, pbuf, coef, cbuf,
+    groups, peers, near_in, far_in, link_in, cols, pts_in, basis_in, up_in, coupling_in,
+    links_in, out, near_pairs, far_mask, link_mask, pts, own, basis, up, coupling, links, slots, xh, xl, pts_t, pown, pbuf, coef, cbuf,
     lift, lift_in, lift_mid, lift_far, gath, part, part_in, part_mid, part_far, far,
     load_sem, s_send, s_recv, p_send, p_recv, c_send, c_recv, pair_send, pair_recv,
     r_send, r_recv, g_send, g_recv, q_send, q_recv, f_send, f_recv,
@@ -56,7 +58,8 @@
         pltpu.make_async_copy(source, target, load_sem.at[n])
         for n, (source, target) in enumerate(
             ((cols, own), (basis_in, basis), (up_in, up), (coupling_in, coupling),
-             (links_in, links))
+             (links_in, links), (pts_in, pts), (near_in, near_pairs), (far_in, far_mask),
+             (link_in, link_mask))
         )
     ]
     for load in loads:
@@ -116,10 +119,14 @@
             device_id_type=MESH,
         ).wait_recv()
 
-    def arrived_all(slot):
-        @pl.loop(0, chunks)
-        def _(k):
-            arrived(slot, k)
+    relayed_outer, relayed_inner = (2, -1, -2), (2, 3)
+
+    def wait_for(condition, offset, half):
+        @pl.when(condition)
+        def _():
+            @pl.loop(half * (chunks // 2), (half + 1) * (chunks // 2))
+            def _(k):
+                arrived(slot_of(offset), k)
 
     def own_outer(k):
         return (
@@ -164,8 +171,8 @@
             def _(k):
                 start_each(own_inner(k))
 
-    ahead = 2
     own_start(0, ahead)
+    loads[5].wait()
     pown[0:3, :] = pts[...]
     pown[3:8, :] = jnp.zeros((5, leaf), f32)
 
@@ -183,8 +190,10 @@
     for offset in near_offsets:
         point_copy(offset).start()
 
-    def split_columns(source):
-        @pl.loop(0, leaf // row_tile)
+    half_rows = leaf // 2
+
+    def split_columns(source, begin, end):
+        @pl.loop(begin // row_tile, end // row_tile)
         def _(t):
             rows = pl.ds(pl.multiple_of(t * row_tile, row_tile), row_tile)
             high, low = halves(source[rows, :])
@@ -192,7 +201,7 @@
             xl[rows, :] = low
 
     loads[0].wait()
-    split_columns(own)
+    split_columns(own, 0, leaf)
     loads[1].wait()
     coef[...] = dot_split_t(halves(basis[...]), (xh[...], xl[...]))
 
@@ -328,7 +337,7 @@
     scatter_pair(dot_split_t(halves(up[...]), halves(coef[...])), lift, 0)
     pts_t[...] = pown[...].T
 
-    def near_product(source, weight, first):
+    def near_product(source, weight, begin, end, first):
         scale = weight * (1.0 / math.sqrt(leaf))
 
         @pl.loop(0, leaf // row_tile)
@@ -336,17 +345,17 @@
             rows = pl.ds(pl.multiple_of(t * row_tile, row_tile), row_tile)
             squared = None
             for axis in range(3):
-                delta = pts_t[rows, axis : axis + 1] - source[axis : axis + 1, :]
+                delta = pts_t[rows, axis : axis + 1] - source[axis : axis + 1, begin:end]
                 delta = delta - jnp.floor(delta + 0.5)
                 squared = delta * delta if squared is None else squared + delta * delta
             block = halves(lax.rsqrt(squared + soften_sq) * scale)
-            value = dot_split(block, (xh[...], xl[...]))
+            value = dot_split(block, (xh[begin:end, :], xl[begin:end, :]))
             if first:
                 out[rows, :] = value
             else:
                 out[rows, :] += value
 
-    near_product(pown, 1.0, True)
+    near_product(pown, 1.0, 0, leaf, True)
 
     def first_relays(begin, end):
         @pl.when(outer)
@@ -365,35 +374,50 @@
                 arrived(slot_of(3), k)
                 first_inner(k)[0].start()
 
-    def add_block(out_offset, in_offset):
+    def add_half(out_offset, in_offset, half):
+        begin = half * half_rows
+        end = begin + half_rows
+        if out_offset not in relayed_outer:
+            wait_for(outer, out_offset, half)
+        if in_offset not in relayed_inner:
+            wait_for(inner, in_offset, half)
         slot = jnp.where(outer, slot_of(out_offset), slot_of(in_offset))
         offset = jnp.where(outer, out_offset, in_offset) * sign
         place_of = jnp.where(offset < 0, offset + 3, offset + 2)
         row = lax.rem(me + jnp.minimum(offset, 0) + leaves, leaves)
         distance = jnp.maximum(offset, -offset)
-        weight = (near_pairs[row, distance - 1] > 0).astype(f32)
-        split_columns(slots.at[slot])
-        near_product(pbuf.at[place_of], weight, False)
-
-    def wait_for(condition, offset):
-        @pl.when(condition)
+        weight = (near_pairs[distance - 1, row] > 0).astype(f32)
+        split_columns(slots.at[slot], begin, end)
+        near_product(pbuf.at[place_of], weight, begin, end, False)
+
+    def later_relays(begin, end):
+        @pl.when(outer)
         def _():
-            arrived_all(slot_of(offset))
-
-    def turn(k):
-        if k + ahead < chunks:
-            own_start(k + ahead, k + ahead + 1)
-        first_relays(k, k + 1)
+            @pl.loop(begin, end)
+            def _(k):
+                copies = later_outer(k)
+                arrived(slot_of(-2), k)
+                copies[0].start()
+                arrived(slot_of(-1), k)
+                copies[1].start()
+
+    def turns(begin, end):
+        for k in range(begin, end):
+            if k + ahead < chunks:
+                own_start(k + ahead, k + ahead + 1)
+            first_relays(k, k + 1)
+            if k >= lag:
+                later_relays(k - lag, k - lag + 1)
 
     scatter_start(lift, lift_in, lift_mid, lift_far, r_send, r_recv, 0)
-    turn(0)
+    turns(0, 1)
     gath[grp] = scatter_end(lift_mid, lift_far, r_send, r_recv)
 
     @pl.loop(1, groups)
     def _(t):
         group_copy(t).start()
 
-    turn(1)
+    turns(1, 3)
     coef_arrived(1 - odd)
     coef_copies[1].start()
 
@@ -401,15 +425,15 @@
     def _(t):
         group_arrived(t)
 
-    for load in loads[3:]:
+    for load in loads[3:5] + loads[6:]:
         load.wait()
     flat = jnp.concatenate(
         [gath[h] * link_mask[0, h].astype(f32) for h in range(groups)], axis=0
     )
     scatter_pair(dot_split_t(halves(links[...]), halves(flat)), part, 1)
-    turn(2)
+    turns(3, 4)
     scatter_start(part, part_in, part_mid, part_far, q_send, q_recv, 1)
-    turn(3)
+    turns(4, 6)
     far[core, chip] = scatter_end(part_mid, part_far, q_send, q_recv)
 
     @pl.loop(1, chips)
@@ -419,38 +443,33 @@
     coef_arrived(odd)
     coef_copies[2].start()
     coef_copies[3].start()
-    turn(4)
+    turns(6, 7)
 
     @pl.loop(1, chips)
     def _(t):
         far_arrived(t)
 
     pair_copies[2].start()
-    turn(5)
+    turns(7, 8)
     for offset in near_offsets:
         point_copy(offset).wait()
-    wait_for(outer, 1)
-    wait_for(inner, -1)
-    add_block(1, -1)
-    for k in range(6, chunks):
-        turn(k)
-    add_block(2, 2)
-
-    @pl.when(outer)
-    def _():
-        @pl.loop(0, chunks)
-        def _(k):
-            copies = later_outer(k)
-            arrived(slot_of(-2), k)
-            copies[0].start()
-            arrived(slot_of(-1), k)
-            copies[1].start()
-
-    wait_for(outer, 3)
-    wait_for(inner, 1)
-    add_block(3, 1)
-    wait_for(outer, -3)
-    add_block(-3, 3)
+    add_half(1, -1, 0)
+    turns(8, 9)
+    add_half(2, 2, 0)
+    turns(9, 11)
+    add_half(3, 1, 0)
+    turns(11, 12)
+    add_half(-3, 3, 0)
+    turns(12, 14)
+    add_half(-1, -2, 0)
+    turns(14, 15)
+    add_half(-2, -3, 0)
+    turns(15, chunks)
+    add_half(1, -1, 1)
+    add_half(2, 2, 1)
+    later_relays(chunks - lag, chunks)
+    add_half(3, 1, 1)
+    add_half(-3, 3, 1)
 
     pair_copies[2].wait_recv()
     for slot in (2, 3):
@@ -466,10 +485,8 @@
         rows = pl.ds(pl.multiple_of(t * row_tile, row_tile), row_tile)
         out[rows, :] += dot_split(halves(basis[rows, :]), total)
 
-    wait_for(inner, -2)
-    add_block(-1, -2)
-    wait_for(inner, -3)
-    add_block(-2, -3)
+    add_half(-1, -2, 1)
+    add_half(-2, -3, 1)
 
     for copy in coef_copies + pair_copies:
         copy.wait_send()
@@ -521,8 +538,7 @@
     up = up.reshape(rank, tall)
     links = links.reshape(groups * padded, tall)
     vmem = pl.BlockSpec(memory_space=pltpu.VMEM)
-    smem = pl.BlockSpec(memory_space=pltpu.SMEM)
-    anywhere = pl.BlockSpec(memory_space=pl.ANY)
+    hbm = pl.BlockSpec(memory_space=pltpu.HBM)
     dma = pltpu.SemaphoreType.DMA
     chips = peers // 2
     slab = pltpu.VMEM((chips, padded, width), f32)
@@ -530,9 +546,13 @@
     return pl.pallas_call(
         functools.partial(body, groups, peers),
         out_shape=jax.ShapeDtypeStruct((leaf, width), f32),
-        in_specs=[smem] * 3 + [anywhere, vmem] + [anywhere] * 4,
+        in_specs=[hbm] * 9,
         out_specs=vmem,
         scratch_shapes=[
+            pltpu.SMEM(near_pairs.shape[::-1], jnp.int32),
+            pltpu.SMEM(far_mask.shape, jnp.int32),
+            pltpu.SMEM(group_link_mask.shape, jnp.int32),
+            pltpu.VMEM(points.shape, f32),
             pltpu.VMEM((leaf, width), f32),
             pltpu.VMEM((leaf, rank), f32),
             pltpu.VMEM((rank, tall), f32),
@@ -556,7 +576,7 @@
             slab,
             slab,
             pair,
-            dma((5,)),
+            dma((9,)),
             dma((7, chunks)),
             dma((6, chunks)),
             dma((6,)),
@@ -575,10 +595,10 @@
             dma((chips,)),
         ],
         compiler_params=pltpu.CompilerParams(
-            collective_id=0, has_side_effects=True, vmem_limit_bytes=48 * 1024 * 1024
+            collective_id=0, has_side_effects=True, vmem_limit_bytes=62 * 1024 * 1024
         ),
     )(
-        near_pairs, far_mask, group_link_mask, columns, points, basis, up, leaf_coupling[0],
+        near_pairs.T, far_mask, group_link_mask, columns, points, basis, up, leaf_coupling[0],
         links,
     )
 

time: 109 us -> 109 us (level)
  Pallas kernels: 99.1 us -> 106 us
  local copies, waits for them, and re-layouts: 8.82 us -> 2.65 us
    pallas_call x1, Pallas kernels: 99.1 us -> 106 us  [per_device(): pl.pallas_call(functools.partial(body, groups, peers), out_shape=jax.Shap...]
    unnamed x18 -> x1, local copies, waits for them, and re-layouts: 8.82 us -> 2.65 us
where the time goes in v1:
time: 109 us
  Pallas kernels  106 us (97%)
  local copies, waits for them, and re-layouts  2.65 us (2%)
    pallas_call x1, Pallas kernels, per_device(): pl.pallas_call(functools.partial(body, groups, peers), out_shape=jax.Shap...  106 us
    unnamed x1, local copies, waits for them, and re-layouts  2.65 us

profile of v1, /device:TPU:0, one launch (start us, length us, event | category | flops | bytes accessed | tf_op | source)
XLA Modules:
  0.0 108.6 jit_solution(11832576027741637460)
XLA Ops:
  0.0 106.0 %shard_map.91 = f32[512,768]{1,0:T(8,128)} custom-call(s32[3,32]{1,0:T(4,128)} %bitcast.7, s32[1,4]{1,0:T(1,128)} %far_in.1, s32[1,4]{1,0:T(1,128)} %link_in.1, f32[512,768]{1,0:T(8,128)} %cols.1, f32[3,512]{1,0:T(4,128)} %pts_in.1, f32[512,128]{1,0:T(8,128)} %basis_in.1, f32[128,128]{1,0:T(8,128)} %bitcast.5, f32[4,128,128]{2,1,0:T(8,128)} %bitcast.4, ...), custom_call_target="tpu_custom_call" | custom-call | tf_op jit(solution)/shard_map/pallas_call | solution.py:546
  106.0 2.7 %copy.11 = f32[512,768]{1,0:T(8,128)} copy(f32[512,768]{1,0:T(8,128)} %shard_map.91) | data formatting | bytes 3145728

commit v2 on v1

--- a/solution.py
+++ b/solution.py
@@ -10,8 +10,8 @@
 
 soften_sq = 0.0025
 chunks = 16
-ahead = 4
-lag = 3
+ahead = 3
+lag = 4
 row_tile = 128
 f32 = jnp.float32
 MESH = pl.DeviceIdType.MESH
@@ -409,17 +409,18 @@
             if k >= lag:
                 later_relays(k - lag, k - lag + 1)
 
+    turns(0, 2)
     scatter_start(lift, lift_in, lift_mid, lift_far, r_send, r_recv, 0)
-    turns(0, 1)
+    turns(2, 4)
     gath[grp] = scatter_end(lift_mid, lift_far, r_send, r_recv)
 
     @pl.loop(1, groups)
     def _(t):
         group_copy(t).start()
 
-    turns(1, 3)
     coef_arrived(1 - odd)
     coef_copies[1].start()
+    turns(4, 6)
 
     @pl.loop(1, groups)
     def _(t):
@@ -431,36 +432,34 @@
         [gath[h] * link_mask[0, h].astype(f32) for h in range(groups)], axis=0
     )
     scatter_pair(dot_split_t(halves(links[...]), halves(flat)), part, 1)
-    turns(3, 4)
+    turns(6, 8)
     scatter_start(part, part_in, part_mid, part_far, q_send, q_recv, 1)
-    turns(4, 6)
-    far[core, chip] = scatter_end(part_mid, part_far, q_send, q_recv)
-
-    @pl.loop(1, chips)
-    def _(t):
-        far_copy(t).start()
-
-    coef_arrived(odd)
-    coef_copies[2].start()
-    coef_copies[3].start()
-    turns(6, 7)
-
-    @pl.loop(1, chips)
-    def _(t):
-        far_arrived(t)
-
-    pair_copies[2].start()
-    turns(7, 8)
     for offset in near_offsets:
         point_copy(offset).wait()
     add_half(1, -1, 0)
     turns(8, 9)
+    coef_arrived(odd)
+    coef_copies[2].start()
+    coef_copies[3].start()
+    turns(9, 10)
+    far[core, chip] = scatter_end(part_mid, part_far, q_send, q_recv)
+
+    @pl.loop(1, chips)
+    def _(t):
+        far_copy(t).start()
+
     add_half(2, 2, 0)
-    turns(9, 11)
+    turns(10, 12)
+
+    @pl.loop(1, chips)
+    def _(t):
+        far_arrived(t)
+
+    pair_copies[2].start()
     add_half(3, 1, 0)
-    turns(11, 12)
+    turns(12, 13)
     add_half(-3, 3, 0)
-    turns(12, 14)
+    turns(13, 14)
     add_half(-1, -2, 0)
     turns(14, 15)
     add_half(-2, -3, 0)

time: 109 us -> 104 us (0.954)
  Pallas kernels: 106 us -> 100 us
    pallas_call x1, Pallas kernels: 106 us -> 100 us  [per_device(): pl.pallas_call(functools.partial(body, groups, peers), out_shape=jax.Shap...]
where the time goes in v2:
time: 104 us; the launch traced here: 103 us
  Pallas kernels  100 us (96%)
  local copies, waits for them, and re-layouts  2.65 us (3%)
    pallas_call x1, Pallas kernels, per_device(): pl.pallas_call(functools.partial(body, groups, peers), out_shape=jax.Shap...  100 us
    unnamed x1, local copies, waits for them, and re-layouts  2.65 us

profile of v2, /device:TPU:0, one launch (start us, length us, event | category | flops | bytes accessed | tf_op | source)
XLA Modules:
  0.0 103.2 jit_solution(10568054502069770998)
XLA Ops:
  0.0 100.5 %shard_map.91 = f32[512,768]{1,0:T(8,128)} custom-call(s32[3,32]{1,0:T(4,128)} %bitcast.7, s32[1,4]{1,0:T(1,128)} %far_in.1, s32[1,4]{1,0:T(1,128)} %link_in.1, f32[512,768]{1,0:T(8,128)} %cols.1, f32[3,512]{1,0:T(4,128)} %pts_in.1, f32[512,128]{1,0:T(8,128)} %basis_in.1, f32[128,128]{1,0:T(8,128)} %bitcast.5, f32[4,128,128]{2,1,0:T(8,128)} %bitcast.4, ...), custom_call_target="tpu_custom_call" | custom-call | tf_op jit(solution)/shard_map/pallas_call | solution.py:545
  100.5 2.7 %copy.11 = f32[512,768]{1,0:T(8,128)} copy(f32[512,768]{1,0:T(8,128)} %shard_map.91) | data formatting | bytes 3145728

commit v3 on v2

--- a/solution.py
+++ b/solution.py
@@ -26,29 +26,31 @@
     return high, (value - high.astype(f32)).astype(jnp.bfloat16)
 
 
-def dot16(left, right):
-    return jnp.dot(left, right, preferred_element_type=f32)
-
-
 def dot_split(left, right):
-    lh, ll = left
-    rh, rl = right
-    return dot16(lh, rh) + dot16(lh, rl) + dot16(ll, rh)
+    lh, ll = halves(left)
+    rh, rl = halves(right)
+    return jnp.dot(
+        jnp.concatenate([lh, ll, lh], axis=1),
+        jnp.concatenate([rh, rh, rl], axis=0),
+        preferred_element_type=f32,
+    )
+
+
+def dot_split_t(left, right):
+    lh, ll = halves(left)
+    rh, rl = halves(right)
+    return dot16_t(
+        jnp.concatenate([lh, ll, lh], axis=0), jnp.concatenate([rh, rh, rl], axis=0)
+    )
 
 
 def dot16_t(left, right):
     return lax.dot_general(left, right, (((0,), (0,)), ((), ())), preferred_element_type=f32)
 
 
-def dot_split_t(left, right):
-    lh, ll = left
-    rh, rl = right
-    return dot16_t(lh, rh) + dot16_t(lh, rl) + dot16_t(ll, rh)
-
-
 def body(
     groups, peers, near_in, far_in, link_in, cols, pts_in, basis_in, up_in, coupling_in,
-    links_in, out, near_pairs, far_mask, link_mask, pts, own, basis, up, coupling, links, slots, xh, xl, pts_t, pown, pbuf, coef, cbuf,
+    links_in, out, near_pairs, far_mask, link_mask, pts, own, basis, up, coupling, links, slots, xcat, kcat, pts_t, pown, pbuf, coef, cbuf,
     lift, lift_in, lift_mid, lift_far, gath, part, part_in, part_mid, part_far, far,
     load_sem, s_send, s_recv, p_send, p_recv, c_send, c_recv, pair_send, pair_recv,
     r_send, r_recv, g_send, g_recv, q_send, q_recv, f_send, f_recv,
@@ -192,18 +194,25 @@
 
     half_rows = leaf // 2
 
-    def split_columns(source, begin, end):
-        @pl.loop(begin // row_tile, end // row_tile)
+    def split_columns(source, begin):
+        @pl.loop(0, half_rows // row_tile)
         def _(t):
-            rows = pl.ds(pl.multiple_of(t * row_tile, row_tile), row_tile)
-            high, low = halves(source[rows, :])
-            xh[rows, :] = high
-            xl[rows, :] = low
+            at = pl.multiple_of(t * row_tile, row_tile)
+            high, low = halves(source[pl.ds(begin + at, row_tile), :])
+            xcat[pl.ds(at, row_tile), :] = high
+            xcat[pl.ds(half_rows + at, row_tile), :] = high
+            xcat[pl.ds(2 * half_rows + at, row_tile), :] = low
+
+    def coef_half(begin):
+        high, low = halves(basis[begin : begin + half_rows, :])
+        return dot16_t(jnp.concatenate([high, low, high], axis=0), xcat[...])
 
     loads[0].wait()
-    split_columns(own, 0, leaf)
     loads[1].wait()
-    coef[...] = dot_split_t(halves(basis[...]), (xh[...], xl[...]))
+    split_columns(own, 0)
+    coef[...] = coef_half(0)
+    split_columns(own, half_rows)
+    coef[...] += coef_half(half_rows)
 
     odd = lax.rem(me // 4, 2)
     toward = 4 - 8 * odd
@@ -334,28 +343,43 @@
         ).wait_recv()
 
     loads[2].wait()
-    scatter_pair(dot_split_t(halves(up[...]), halves(coef[...])), lift, 0)
+    scatter_pair(dot_split_t(up[...], coef[...]), lift, 0)
     pts_t[...] = pown[...].T
 
-    def near_product(source, weight, begin, end, first):
+    column_tile = 256 if width % 256 == 0 else width
+
+    def near_product(source, shift, weight, begin, first):
         scale = weight * (1.0 / math.sqrt(leaf))
+        end = begin + half_rows
+        coords = [source[axis : axis + 1, begin:end] for axis in range(3)]
+        coords[0] = coords[0] + shift
 
         @pl.loop(0, leaf // row_tile)
         def _(t):
             rows = pl.ds(pl.multiple_of(t * row_tile, row_tile), row_tile)
-            squared = None
-            for axis in range(3):
-                delta = pts_t[rows, axis : axis + 1] - source[axis : axis + 1, begin:end]
+            delta = pts_t[rows, 0:1] - coords[0]
+            squared = delta * delta
+            for axis in (1, 2):
+                delta = pts_t[rows, axis : axis + 1] - coords[axis]
                 delta = delta - jnp.floor(delta + 0.5)
-                squared = delta * delta if squared is None else squared + delta * delta
-            block = halves(lax.rsqrt(squared + soften_sq) * scale)
-            value = dot_split(block, (xh[begin:end, :], xl[begin:end, :]))
+                squared = squared + delta * delta
+            high, low = halves(lax.rsqrt(squared + soften_sq) * scale)
+            kcat[rows, 0:half_rows] = high
+            kcat[rows, half_rows : 2 * half_rows] = low
+            kcat[rows, 2 * half_rows : 3 * half_rows] = high
+
+        @pl.loop(0, width // column_tile)
+        def _(t):
+            at = pl.ds(pl.multiple_of(t * column_tile, column_tile), column_tile)
+            value = jnp.dot(kcat[...], xcat[:, at], preferred_element_type=f32)
             if first:
-                out[rows, :] = value
+                out[:, at] = value
             else:
-                out[rows, :] += value
-
-    near_product(pown, 1.0, 0, leaf, True)
+                out[:, at] += value
+
+    near_product(pown, 0.0, 1.0, half_rows, True)
+    split_columns(own, 0)
+    near_product(pown, 0.0, 1.0, 0, False)
 
     def first_relays(begin, end):
         @pl.when(outer)
@@ -376,7 +400,6 @@
 
     def add_half(out_offset, in_offset, half):
         begin = half * half_rows
-        end = begin + half_rows
         if out_offset not in relayed_outer:
             wait_for(outer, out_offset, half)
         if in_offset not in relayed_inner:
@@ -387,8 +410,10 @@
         row = lax.rem(me + jnp.minimum(offset, 0) + leaves, leaves)
         distance = jnp.maximum(offset, -offset)
         weight = (near_pairs[distance - 1, row] > 0).astype(f32)
-        split_columns(slots.at[slot], begin, end)
-        near_product(pbuf.at[place_of], weight, begin, end, False)
+        split_columns(slots.at[slot], begin)
+        beyond = me + offset
+        shift = jnp.where(beyond >= leaves, 1.0, jnp.where(beyond < 0, -1.0, 0.0))
+        near_product(pbuf.at[place_of], shift, weight, begin, False)
 
     def later_relays(begin, end):
         @pl.when(outer)
@@ -431,7 +456,7 @@
     flat = jnp.concatenate(
         [gath[h] * link_mask[0, h].astype(f32) for h in range(groups)], axis=0
     )
-    scatter_pair(dot_split_t(halves(links[...]), halves(flat)), part, 1)
+    scatter_pair(dot_split_t(links[...], flat), part, 1)
     turns(6, 8)
     scatter_start(part, part_in, part_mid, part_far, q_send, q_recv, 1)
     for offset in near_offsets:
@@ -474,15 +499,18 @@
     for slot in (2, 3):
         coef_arrived(slot)
     raised = jnp.stack([far[0], far[1]], axis=1).reshape(up.shape[1], width)
-    total = dot_split(halves(up[...]), halves(raised))
+    total = dot_split(up[...], raised)
     for entry in range(4):
-        total += far_mask[0, entry].astype(f32) * dot_split(halves(coupling[entry]), halves(cbuf[entry]))
-    total = halves(total)
+        total += far_mask[0, entry].astype(f32) * dot_split(coupling[entry], cbuf[entry])
+    high, low = halves(total)
+    total = jnp.concatenate([high, high, low], axis=0)
 
     @pl.loop(0, leaf // row_tile)
     def _(t):
         rows = pl.ds(pl.multiple_of(t * row_tile, row_tile), row_tile)
-        out[rows, :] += dot_split(halves(basis[rows, :]), total)
+        high, low = halves(basis[rows, :])
+        left = jnp.concatenate([high, low, high], axis=1)
+        out[rows, :] += jnp.dot(left, total, preferred_element_type=f32)
 
     add_half(-1, -2, 1)
     add_half(-2, -3, 1)
@@ -558,8 +586,8 @@
             pltpu.VMEM(leaf_coupling.shape[1:], f32),
             pltpu.VMEM((groups * padded, tall), f32),
             pltpu.VMEM((6, leaf, width), f32),
-            pltpu.VMEM((leaf, width), jnp.bfloat16),
-            pltpu.VMEM((leaf, width), jnp.bfloat16),
+            pltpu.VMEM((3 * leaf // 2, width), jnp.bfloat16),
+            pltpu.VMEM((leaf, 3 * leaf // 2), jnp.bfloat16),
             pltpu.VMEM((leaf, 8), f32),
             pltpu.VMEM((8, leaf), f32),
             pltpu.VMEM((6, 8, leaf), f32),

time: 104 us -> 104 us (level)
  no operation moved by 1% of the time
where the time goes in v3:
time: 104 us
  Pallas kernels  101 us (97%)
  local copies, waits for them, and re-layouts  2.65 us (3%)
    pallas_call x1, Pallas kernels, per_device(): pl.pallas_call(functools.partial(body, groups, peers), out_shape=jax.Shap...  101 us
    unnamed x1, local copies, waits for them, and re-layouts  2.65 us

profile of v3, /device:TPU:0, one launch (start us, length us, event | category | flops | bytes accessed | tf_op | source)
XLA Modules:
  0.0 103.7 jit_solution(7151707262385876008)
XLA Ops:
  0.0 101.1 %shard_map.91 = f32[512,768]{1,0:T(8,128)} custom-call(s32[3,32]{1,0:T(4,128)} %bitcast.7, s32[1,4]{1,0:T(1,128)} %far_in.1, s32[1,4]{1,0:T(1,128)} %link_in.1, f32[512,768]{1,0:T(8,128)} %cols.1, f32[3,512]{1,0:T(4,128)} %pts_in.1, f32[512,128]{1,0:T(8,128)} %basis_in.1, f32[128,128]{1,0:T(8,128)} %bitcast.5, f32[4,128,128]{2,1,0:T(8,128)} %bitcast.4, ...), custom_call_target="tpu_custom_call" | custom-call | tf_op jit(solution)/shard_map/pallas_call | solution.py:573
  101.1 2.7 %copy.11 = f32[512,768]{1,0:T(8,128)} copy(f32[512,768]{1,0:T(8,128)} %shard_map.91) | data formatting | bytes 3145728

commit v4 on v3

--- a/solution.py
+++ b/solution.py
@@ -10,8 +10,8 @@
 
 soften_sq = 0.0025
 chunks = 16
-ahead = 3
-lag = 4
+ahead = 6
+lag = 5
 row_tile = 128
 f32 = jnp.float32
 MESH = pl.DeviceIdType.MESH
@@ -80,7 +80,7 @@
         return (index // peers, lax.rem(index, peers))
 
     barrier = pltpu.get_barrier_semaphore()
-    for offset in (-8, -4, -3, -2, -1, 1, 2, 3, 4, 8):
+    for offset in (-8, -5, -4, -3, -2, -1, 1, 2, 3, 4, 5, 8):
         pl.semaphore_signal(barrier, inc=1, device_id=device(me + offset), device_id_type=MESH)
 
     @pl.loop(1, peers)
@@ -95,7 +95,7 @@
             barrier, inc=1, device_id=(lax.rem(grp + t, groups), dev), device_id_type=MESH
         )
 
-    pl.semaphore_wait(barrier, 10 + peers - 1 + groups - 1)
+    pl.semaphore_wait(barrier, 12 + peers - 1 + groups - 1)
 
     def piece(k):
         return pl.ds(pl.multiple_of(k * step, step), step)
@@ -230,10 +230,32 @@
     coef_copies = (
         coef_copy(coef, 0, odd, toward),
         coef_copy(cbuf.at[1 - odd], 1, odd, 2 * toward),
-        coef_copy(cbuf.at[0], 2, 2, 1),
-        coef_copy(cbuf.at[1], 3, 3, -1),
-    )
+    )
+    rises, falls = place == 3, place == 0
+
+    def far_coef(channel):
+        leap, to = ((rises, 1), (falls, -1))[channel - 2]
+        return leap, coef_copy(coef, channel, channel, 5 * to), coef_copy(
+            cbuf.at[channel - 2], channel, channel, to
+        )
+
+    def leap_start(channel):
+        leap, direct, _ = far_coef(channel)
+
+        @pl.when(leap)
+        def _():
+            direct.start()
+
+    def step_start(channel):
+        leap, _, via = far_coef(channel)
+
+        @pl.when(jnp.logical_not(leap))
+        def _():
+            via.start()
+
     coef_copies[0].start()
+    leap_start(2)
+    leap_start(3)
 
     def coef_arrived(slot):
         coef_copy(coef, 0, slot, 1).wait_recv()
@@ -464,8 +486,8 @@
     add_half(1, -1, 0)
     turns(8, 9)
     coef_arrived(odd)
-    coef_copies[2].start()
-    coef_copies[3].start()
+    step_start(2)
+    step_start(3)
     turns(9, 10)
     far[core, chip] = scatter_end(part_mid, part_far, q_send, q_recv)
 
@@ -515,7 +537,7 @@
     add_half(-1, -2, 1)
     add_half(-2, -3, 1)
 
-    for copy in coef_copies + pair_copies:
+    for copy in coef_copies + pair_copies + (far_coef(2)[1], far_coef(3)[1]):
         copy.wait_send()
 
     @pl.loop(1, chips)

time: 104 us -> 102 us (0.981)
  Pallas kernels: 101 us -> 99.6 us
    pallas_call x1, Pallas kernels: 101 us -> 99.6 us  [per_device(): pl.pallas_call(functools.partial(body, groups, peers), out_shape=jax.Shap...]
where the time goes in v4:
time: 102 us
  Pallas kernels  99.6 us (98%)
  local copies, waits for them, and re-layouts  2.65 us (3%)
    pallas_call x1, Pallas kernels, per_device(): pl.pallas_call(functools.partial(body, groups, peers), out_shape=jax.Shap...  99.6 us
    unnamed x1, local copies, waits for them, and re-layouts  2.65 us

profile of v4, /device:TPU:0, one launch (start us, length us, event | category | flops | bytes accessed | tf_op | source)
XLA Modules:
  0.0 102.2 jit_solution(287040739807659975)
XLA Ops:
  0.0 99.6 %shard_map.91 = f32[512,768]{1,0:T(8,128)} custom-call(s32[3,32]{1,0:T(4,128)} %bitcast.7, s32[1,4]{1,0:T(1,128)} %far_in.1, s32[1,4]{1,0:T(1,128)} %link_in.1, f32[512,768]{1,0:T(8,128)} %cols.1, f32[3,512]{1,0:T(4,128)} %pts_in.1, f32[512,128]{1,0:T(8,128)} %basis_in.1, f32[128,128]{1,0:T(8,128)} %bitcast.5, f32[4,128,128]{2,1,0:T(8,128)} %bitcast.4, ...), custom_call_target="tpu_custom_call" | custom-call | tf_op jit(solution)/shard_map/pallas_call | solution.py:595
  99.6 2.7 %copy.11 = f32[512,768]{1,0:T(8,128)} copy(f32[512,768]{1,0:T(8,128)} %shard_map.91) | data formatting | bytes 3145728

commit v5 on v4

--- a/solution.py
+++ b/solution.py
@@ -509,14 +509,6 @@
     turns(13, 14)
     add_half(-1, -2, 0)
     turns(14, 15)
-    add_half(-2, -3, 0)
-    turns(15, chunks)
-    add_half(1, -1, 1)
-    add_half(2, 2, 1)
-    later_relays(chunks - lag, chunks)
-    add_half(3, 1, 1)
-    add_half(-3, 3, 1)
-
     pair_copies[2].wait_recv()
     for slot in (2, 3):
         coef_arrived(slot)
@@ -533,6 +525,16 @@
         high, low = halves(basis[rows, :])
         left = jnp.concatenate([high, low, high], axis=1)
         out[rows, :] += jnp.dot(left, total, preferred_element_type=f32)
+
+    add_half(-2, -3, 0)
+    turns(15, chunks)
+    later_relays(chunks - lag, chunks - 3)
+    add_half(1, -1, 1)
+    later_relays(chunks - 3, chunks - 1)
+    add_half(2, 2, 1)
+    later_relays(chunks - 1, chunks)
+    add_half(3, 1, 1)
+    add_half(-3, 3, 1)
 
     add_half(-1, -2, 1)
     add_half(-2, -3, 1)

time: 102 us -> 102 us (level)
  no operation moved by 1% of the time
where the time goes in v5:
time: 102 us
  Pallas kernels  99.6 us (98%)
  local copies, waits for them, and re-layouts  2.65 us (3%)
    pallas_call x1, Pallas kernels, per_device(): pl.pallas_call(functools.partial(body, groups, peers), out_shape=jax.Shap...  99.6 us
    unnamed x1, local copies, waits for them, and re-layouts  2.65 us

profile of v5, /device:TPU:0, one launch (start us, length us, event | category | flops | bytes accessed | tf_op | source)
XLA Modules:
  0.0 102.2 jit_solution(12715799923129340658)
XLA Ops:
  0.0 99.6 %shard_map.91 = f32[512,768]{1,0:T(8,128)} custom-call(s32[3,32]{1,0:T(4,128)} %bitcast.7, s32[1,4]{1,0:T(1,128)} %far_in.1, s32[1,4]{1,0:T(1,128)} %link_in.1, f32[512,768]{1,0:T(8,128)} %cols.1, f32[3,512]{1,0:T(4,128)} %pts_in.1, f32[512,128]{1,0:T(8,128)} %basis_in.1, f32[128,128]{1,0:T(8,128)} %bitcast.5, f32[4,128,128]{2,1,0:T(8,128)} %bitcast.4, ...), custom_call_target="tpu_custom_call" | custom-call | tf_op jit(solution)/shard_map/pallas_call | solution.py:597
  99.6 2.7 %copy.11 = f32[512,768]{1,0:T(8,128)} copy(f32[512,768]{1,0:T(8,128)} %shard_map.91) | data formatting | bytes 3145728
